TPU v7x, 32 devices: a whole 2x2x4 slice. The times are simulated.
32 devices in a mesh: depth: 8 (over z, y), lat: 4 (over x, core).
Axes of the slice: x: 2, y: 2, z: 4, core: 2. Of those that a mesh axis runs over, the one named last changes fastest.
Arguments:
- densities: float32 [4, 256, 64], P('lat', 'depth'), may hold values from -6 to 6
- source: float32 [4, 256, 64], P('lat', 'depth'), may hold values from -6 to 6
- jacobian: float32 [4, 256, 4096], P('lat', 'depth'), may hold values from -0.75 to 0.75
- pattern: int32 [8, 8], replicated, may hold values 0 or 1
- transport: float32 [4, 256, 64], P('lat', 'depth'), may hold values from 0.2 to 1
- lateral: float32 [4, 256, 64], P('lat', 'depth'), may hold values from 0.1 to 1
- neighbours: int32 [4, 4], P('lat'), may hold values from 0 to 3, as said below
- factor: float32 [4, 256, 4096], P('lat', 'depth'), may hold values from -0.0009765625 to 0.001953125
- coupling: float32 [4, 256, 64], P('lat', 'depth'), may hold values from 512 to 2048
Outputs:
- correction: float32 [4, 256, 64], P('lat', 'depth')
Inputs may be any that keep to these rules, and one draw needn't show every extreme that they name: Each line's four neighbours (previous row, next row, previous place, next place) in a periodic arrangement of the lines in rows of 4, under a relabelling of the lines drawn from the seed.
All inputs are finite; a program needn't handle non-finite values.
Results may differ from a plain program's by a relative error of at most 0.0003.
Values sent between devices are 32-bit elements; how exact they have to be, the bound alone decides.
A program may use at most 128 MiB of HBM per device.

v0:
```python
import jax
import jax.numpy as jnp
from jax import lax
from jax.sharding import PartitionSpec as P

highest = lax.Precision.HIGHEST


def passed_along(value, axis, steps):
    count = lax.axis_size(axis)
    first, last = (max(0, -steps), min(count, count - steps))
    return lax.ppermute(value, axis, [(source, source + steps) for source in range(first, last)])


def compose(earlier, later):
    first_mat, first_vec = earlier
    last_mat, last_vec = later
    joined = jnp.einsum("...ij,...jk->...ik", last_mat, first_mat, precision=highest)
    carried = jnp.einsum("...ij,...j->...i", last_mat, first_vec, precision=highest)
    return (joined, carried + last_vec)


def apply_map(matrix, vector):
    return jnp.einsum("...ij,...j->...i", matrix, vector, precision=highest)


def doubling_prefix(combine, elems, unit, axis, reverse):
    length = jax.tree.leaves(elems)[0].shape[axis]
    stride = 1
    while stride < length:

        def shifted(values, single):
            filler = jnp.repeat(single, stride, axis=axis)
            if reverse:
                return jnp.concatenate(
                    [lax.slice_in_dim(values, stride, length, axis=axis), filler], axis=axis
                )
            return jnp.concatenate(
                [filler, lax.slice_in_dim(values, 0, length - stride, axis=axis)], axis=axis
            )

        earlier = jax.tree.map(shifted, elems, unit)
        elems = combine(earlier, elems)
        stride = stride * 2
    return elems


def on_device(
    densities, source, jacobian, pattern, transport, lateral, neighbours, factor, coupling
):
    line_count, cell_count, species = densities.shape
    tile_size = species // pattern.shape[0]
    depth_count = lax.axis_size("depth")
    mask = jnp.repeat(jnp.repeat(pattern, tile_size, axis=0), tile_size, axis=1).astype(jnp.float32)
    inverses = factor.reshape(line_count, cell_count, species, species)
    forward_mats = coupling[:, :, :, None] * inverses
    backward_mats = inverses * coupling[:, :, None, :]
    identity = jnp.broadcast_to(jnp.eye(species, dtype=jnp.float32), (line_count, species, species))
    empty_vec = jnp.zeros((line_count, species), jnp.float32)
    cell_unit = (identity[:, None], empty_vec[:, None])
    all_lines = lax.all_gather(densities, "lat", axis=0, tiled=True)
    flux = transport * densities
    from_lower = passed_along(flux[:, -1:, :], "depth", 1)
    from_upper = passed_along(densities[:, :1, :], "depth", -1)
    blocks = jacobian.reshape(line_count, cell_count, species, species) * mask
    reaction = jnp.einsum("lkij,lkj->lki", blocks, densities, precision=highest)
    lower_flux = jnp.concatenate([from_lower, flux[:, :-1, :]], axis=1)
    upper_cells = jnp.concatenate([densities[:, 1:, :], from_upper], axis=1)
    neighbour_sum = jnp.sum(all_lines[neighbours], axis=1)
    operator = (
        reaction
        - lower_flux
        - transport * upper_cells
        + lateral * (4.0 * densities - neighbour_sum)
    )
    residual = source - operator
    pivoted = apply_map(inverses, residual)
    prefix_mats, prefix_vecs = doubling_prefix(
        compose, (forward_mats, coupling * pivoted), cell_unit, 1, False
    )
    block_mat = prefix_mats[:, -1]
    block_vec = prefix_vecs[:, -1]

    def forward_turn(counter, carried):
        return passed_along(apply_map(block_mat, carried) + block_vec, "depth", 1)

    incoming = lax.fori_loop(0, depth_count - 1, forward_turn, empty_vec)
    passed = apply_map(prefix_mats, incoming[:, None, :]) + prefix_vecs
    previous = jnp.concatenate([incoming[:, None, :], passed[:, :-1, :]], axis=1)
    forward_vals = pivoted + apply_map(inverses, previous)
    suffix_mats, suffix_vecs = doubling_prefix(
        compose, (backward_mats, forward_vals), cell_unit, 1, True
    )
    head_mat = suffix_mats[:, 0]
    head_vec = suffix_vecs[:, 0]

    def backward_turn(counter, carried):
        return passed_along(apply_map(head_mat, carried) + head_vec, "depth", -1)

    arriving = lax.fori_loop(0, depth_count - 1, backward_turn, empty_vec)
    return apply_map(suffix_mats, arriving[:, None, :]) + suffix_vecs


def solution(mesh):
    return jax.shard_map(
        on_device,
        mesh=mesh,
        in_specs=(
            P("lat", "depth", None),
            P("lat", "depth", None),
            P("lat", "depth", None),
            P(),
            P("lat", "depth", None),
            P("lat", "depth", None),
            P("lat", None),
            P("lat", "depth", None),
            P("lat", "depth", None),
        ),
        out_specs=P("lat", "depth", None),
        check_vma=False,
    )
```

profile of v0, /device:TPU:0, one launch (start us, length us, event | category | flops | bytes accessed | tf_op | source)
XLA Modules:
  0.0 152.4 jit_solution(11330510705622593111)
XLA Ops:
  0.0 0.7 slice.96
  0.7 1.3 collective-permute-start.3
  2.0 0.7 mul.82
  2.7 5.5 %collective-permute-start.2 = (f32[1,1,64]{2,1,0:T(1,128)S(1)}, f32[1,1,64]{2,1,0:T(1,128)S(1)}, u32[]{:S(2)}, u32[]{:S(2)}) collective-permute-start(f32[1,1,64]{2,1,0:T(1,128)S(1)} %slice.125), channel_id=1, source_target_pairs={{0,4},{4,8},{8,12},{12,16},{16,20},{20,24},{24,28},{1,5},{5,9},{9,... | collective-permute-start | bytes 776 | tf_op jit(solution)/shard_map/ppermute | solution.py:12
  8.3 5.2 %all_gather.3 = f32[4,32,64]{2,1,0:T(8,128)S(1)} all-gather(f32[1,32,64]{2,1,0:T(8,128)S(1)} %copy-done.20), channel_id=1, replica_groups=mesh['depth'=8,'lat'=4] {'lat'}, dimensions={0}, use_global_device_ids=true | all-gather | bytes 40960 | tf_op jit(solution)/shard_map/all_gather | solution.py:61
  13.5 1.5 reshape.273
  15.8 0.7 copy-done.24
  17.4 1.5 reshape.284
  19.2 1.3 fusion.23
  20.5 1.2 fusion.8
  21.8 1.2 fusion.26
  23.1 1.2 fusion.29
  24.4 1.2 fusion.32
  25.7 1.2 fusion.35
  27.0 1.2 fusion.11
  28.3 1.4 fusion.14
  29.8 1.2 fusion.17
  31.1 1.2 fusion.20
  32.3 1.0 copy-done.12
  33.3 1.7 %fusion.38 = f32[32,1,64]{2,1,0:T(1,128)S(1)} fusion(f32[32,64,1]{1,2,0:T(1,128)S(1)} %bitcast.297, f32[32,64,64]{2,1,0:T(8,128)S(1)} %copy-done.16, f32[64,64]{1,0:T(8,128)S(1)} %copy.13), kind=kOutput, calls=%fused_computation.51 | convolution fusion | flops 1703936 | bytes 557056 | tf_op jit(solution)/shard_map/lkij,lkj->lki/dot_general | solution.py:66
  36.4 1.7 %fusion.74 = f32[32,1,64]{2,1,0:T(1,128)S(1)} fusion(f32[32,64,1]{1,2,0:T(1,128)S(1)} %bitcast.309, f32[32,64,64]{2,1,0:T(8,128)S(1)} %reshape.273), kind=kOutput, calls=%fused_computation.111 | convolution fusion | flops 1572864 | bytes 540672 | tf_op jit(solution)/shard_map/...ij,...j->...i/dot_general | solution.py:24
  38.1 1.8 %fusion.40 = f32[32,1,64]{2,1,0:T(1,128)S(1)} fusion(f32[32,64,1]{1,2,0:T(1,128)S(1)} %bitcast.333, f32[32,64,64]{2,1,0:T(8,128)S(1)} %reshape.273, f32[32,64]{1,0:T(8,128)S(1)} %bitcast.295), kind=kOutput, calls=%fused_computation.55 | convolution fusion | flops 1703936 | bytes 548864 | tf_op jit(solution)/shard_map/...ij,...j->...i/dot_general | solution.py:19
  40.0 1.7 %fusion.75 = f32[32,1,64]{2,1,0:T(1,128)S(1)} fusion(f32[32,64,64]{2,1,0:T(8,128)S(1)} %fusion.23, f32[32,64,1]{1,2,0:T(1,128)S(1)} %bitcast.331), kind=kOutput, calls=%fused_computation.112 | convolution fusion | flops 1572864 | bytes 540672 | tf_op jit(solution)/shard_map/...ij,...j->...i/dot_general | solution.py:19
  41.8 1.7 %fusion.76 = f32[32,1,64]{2,1,0:T(1,128)S(1)} fusion(f32[32,64,64]{2,1,0:T(8,128)S(1)} %copy-done.3, f32[32,64,1]{1,2,0:T(1,128)S(1)} %bitcast.332), kind=kOutput, calls=%fused_computation.113 | convolution fusion | flops 1572864 | bytes 540672 | tf_op jit(solution)/shard_map/...ij,...j->...i/dot_general | solution.py:19
  43.6 1.7 %fusion.77 = f32[32,1,64]{2,1,0:T(1,128)S(1)} fusion(f32[32,64,64]{2,1,0:T(8,128)S(1)} %copy-done.7, f32[32,64,1]{1,2,0:T(1,128)S(1)} %bitcast.323), kind=kOutput, calls=%fused_computation.114 | convolution fusion | flops 1572864 | bytes 540672 | tf_op jit(solution)/shard_map/...ij,...j->...i/dot_general | solution.py:19
  45.3 1.7 %fusion.78 = f32[32,1,64]{2,1,0:T(1,128)S(1)} fusion(f32[32,64,64]{2,1,0:T(8,128)S(1)} %copy-done.11, f32[32,64,1]{1,2,0:T(1,128)S(1)} %bitcast.325), kind=kOutput, calls=%fused_computation.115 | convolution fusion | flops 1572864 | bytes 540672 | tf_op jit(solution)/shard_map/...ij,...j->...i/dot_general | solution.py:19
  47.1 43.0 %while.20 = (s32[]{:T(128)}, f32[1,64]{1,0:T(1,128)S(1)}, f32[1,64,64]{2,1,0:T(8,128)S(1)}, f32[1,64]{1,0:T(1,128)S(1)}, s32[]{:T(128)}) while((s32[]{:T(128)}, f32[1,64]{1,0:T(1,128)S(1)}, f32[1,64,64]{2,1,0:T(8,128)S(1)}, f32[1,64]{1,0:T(1,128)S(1)}, s32[]{:T(128)}) %tuple.33), condition=%wide.region_2.0_spmd, body=%wide.region_1.0_spmd.sunk | while | flops 49218 | bytes 18277 | solution.py:87
  47.5 4.8 %collective-permute-start = (f32[1,64]{1,0:T(1,128)S(1)}, f32[1,64]{1,0:T(1,128)S(1)}, u32[]{:S(2)}, u32[]{:S(2)}) collective-permute-start(f32[1,64]{1,0:T(1,128)S(1)} %fusion.125), channel_id=1, source_target_pairs={{0,4},{4,8},{8,12},{12,16},{16,20},{20,24},{24,28},{1,5},{5,9},{9,... | collective-permute-start | bytes 776 | tf_op jit(solution)/shard_map/while/body/eval_jaxpr/ppermute | solution.py:12
  52.3 1.3 collective-permute-done
  53.7 4.2 %collective-permute-start = (f32[1,64]{1,0:T(1,128)S(1)}, f32[1,64]{1,0:T(1,128)S(1)}, u32[]{:S(2)}, u32[]{:S(2)}) collective-permute-start(f32[1,64]{1,0:T(1,128)S(1)} %fusion.125), channel_id=1, source_target_pairs={{0,4},{4,8},{8,12},{12,16},{16,20},{20,24},{24,28},{1,5},{5,9},{9,... | collective-permute-start | bytes 776 | tf_op jit(solution)/shard_map/while/body/eval_jaxpr/ppermute | solution.py:12
  57.9 1.3 collective-permute-done
  59.3 4.2 %collective-permute-start = (f32[1,64]{1,0:T(1,128)S(1)}, f32[1,64]{1,0:T(1,128)S(1)}, u32[]{:S(2)}, u32[]{:S(2)}) collective-permute-start(f32[1,64]{1,0:T(1,128)S(1)} %fusion.125), channel_id=1, source_target_pairs={{0,4},{4,8},{8,12},{12,16},{16,20},{20,24},{24,28},{1,5},{5,9},{9,... | collective-permute-start | bytes 776 | tf_op jit(solution)/shard_map/while/body/eval_jaxpr/ppermute | solution.py:12
  63.5 1.3 collective-permute-done
  64.9 4.3 %collective-permute-start = (f32[1,64]{1,0:T(1,128)S(1)}, f32[1,64]{1,0:T(1,128)S(1)}, u32[]{:S(2)}, u32[]{:S(2)}) collective-permute-start(f32[1,64]{1,0:T(1,128)S(1)} %fusion.125), channel_id=1, source_target_pairs={{0,4},{4,8},{8,12},{12,16},{16,20},{20,24},{24,28},{1,5},{5,9},{9,... | collective-permute-start | bytes 776 | tf_op jit(solution)/shard_map/while/body/eval_jaxpr/ppermute | solution.py:12
  69.3 1.3 collective-permute-done
  70.7 5.1 %collective-permute-start = (f32[1,64]{1,0:T(1,128)S(1)}, f32[1,64]{1,0:T(1,128)S(1)}, u32[]{:S(2)}, u32[]{:S(2)}) collective-permute-start(f32[1,64]{1,0:T(1,128)S(1)} %fusion.125), channel_id=1, source_target_pairs={{0,4},{4,8},{8,12},{12,16},{16,20},{20,24},{24,28},{1,5},{5,9},{9,... | collective-permute-start | bytes 776 | tf_op jit(solution)/shard_map/while/body/eval_jaxpr/ppermute | solution.py:12
  75.8 1.3 collective-permute-done
  77.2 5.1 %collective-permute-start = (f32[1,64]{1,0:T(1,128)S(1)}, f32[1,64]{1,0:T(1,128)S(1)}, u32[]{:S(2)}, u32[]{:S(2)}) collective-permute-start(f32[1,64]{1,0:T(1,128)S(1)} %fusion.125), channel_id=1, source_target_pairs={{0,4},{4,8},{8,12},{12,16},{16,20},{20,24},{24,28},{1,5},{5,9},{9,... | collective-permute-start | bytes 776 | tf_op jit(solution)/shard_map/while/body/eval_jaxpr/ppermute | solution.py:12
  82.3 1.3 collective-permute-done
  83.7 5.1 %collective-permute-start = (f32[1,64]{1,0:T(1,128)S(1)}, f32[1,64]{1,0:T(1,128)S(1)}, u32[]{:S(2)}, u32[]{:S(2)}) collective-permute-start(f32[1,64]{1,0:T(1,128)S(1)} %fusion.125), channel_id=1, source_target_pairs={{0,4},{4,8},{8,12},{12,16},{16,20},{20,24},{24,28},{1,5},{5,9},{9,... | collective-permute-start | bytes 776 | tf_op jit(solution)/shard_map/while/body/eval_jaxpr/ppermute | solution.py:12
  88.8 1.3 collective-permute-done
  90.1 2.5 %fusion.61 = f32[1,32,64]{2,0,1:T(1,128)S(1)} fusion(f32[32,64,64]{2,1,0:T(8,128)S(1)} %copy-done.15, f32[1,64]{1,0:T(1,128)S(1)} %get-tuple-element.49), kind=kOutput, calls=%fused_computation.98 | convolution fusion | flops 1572864 | bytes 532736 | tf_op jit(solution)/shard_map/...ij,...j->...i/dot_general | solution.py:24
  92.6 1.7 %fusion.79 = f32[32,1,64]{2,1,0:T(1,128)S(1)} fusion(f32[32,64,1]{1,2,0:T(1,128)S(1)} %bitcast.326, f32[32,64,64]{2,1,0:T(8,128)S(1)} %reshape.273), kind=kOutput, calls=%fused_computation.116 | convolution fusion | flops 1572864 | bytes 540672 | tf_op jit(solution)/shard_map/...ij,...j->...i/dot_general | solution.py:24
  94.4 1.7 %fusion.43 = f32[32,1,64]{2,1,0:T(1,128)S(1)} fusion(f32[32,64,1]{1,2,0:T(1,128)S(1)} %bitcast.327, f32[32,64,64]{2,1,0:T(8,128)S(1)} %reshape.273, f32[32,64]{1,0:T(8,128)S(1)} %bitcast.296), kind=kOutput, calls=%fused_computation.58 | convolution fusion | flops 1703936 | bytes 548864 | tf_op jit(solution)/shard_map/...ij,...j->...i/dot_general | solution.py:19
  96.2 1.7 %fusion.80 = f32[32,1,64]{2,1,0:T(1,128)S(1)} fusion(f32[32,64,64]{2,1,0:T(8,128)S(1)} %fusion.8, f32[32,64,1]{1,2,0:T(1,128)S(1)} %bitcast.328), kind=kOutput, calls=%fused_computation.117 | convolution fusion | flops 1572864 | bytes 540672 | tf_op jit(solution)/shard_map/...ij,...j->...i/dot_general | solution.py:19
  98.0 1.7 %fusion.81 = f32[32,1,64]{2,1,0:T(1,128)S(1)} fusion(f32[32,64,64]{2,1,0:T(8,128)S(1)} %copy-done.1, f32[32,64,1]{1,2,0:T(1,128)S(1)} %bitcast.329), kind=kOutput, calls=%fused_computation.118 | convolution fusion | flops 1572864 | bytes 540672 | tf_op jit(solution)/shard_map/...ij,...j->...i/dot_general | solution.py:19
  99.8 1.7 %fusion.82 = f32[32,1,64]{2,1,0:T(1,128)S(1)} fusion(f32[32,64,64]{2,1,0:T(8,128)S(1)} %copy-done.5, f32[32,64,1]{1,2,0:T(1,128)S(1)} %bitcast.324), kind=kOutput, calls=%fused_computation.119 | convolution fusion | flops 1572864 | bytes 540672 | tf_op jit(solution)/shard_map/...ij,...j->...i/dot_general | solution.py:19
  101.5 1.7 %fusion.83 = f32[32,1,64]{2,1,0:T(1,128)S(1)} fusion(f32[32,64,64]{2,1,0:T(8,128)S(1)} %copy-done.9, f32[32,64,1]{1,2,0:T(1,128)S(1)} %bitcast.330), kind=kOutput, calls=%fused_computation.120 | convolution fusion | flops 1572864 | bytes 540672 | tf_op jit(solution)/shard_map/...ij,...j->...i/dot_general | solution.py:19
  103.3 46.0 %while.21 = (s32[]{:T(128)}, f32[1,64]{1,0:T(1,128)S(1)}, f32[1,64,64]{2,1,0:T(8,128)S(1)}, f32[1,64]{1,0:T(1,128)S(1)}, s32[]{:T(128)}) while((s32[]{:T(128)}, f32[1,64]{1,0:T(1,128)S(1)}, f32[1,64,64]{2,1,0:T(8,128)S(1)}, f32[1,64]{1,0:T(1,128)S(1)}, s32[]{:T(128)}) %tuple.36), condition=%wide.region_4.0_spmd, body=%wide.region_3.0_spmd.sunk | while | flops 49218 | bytes 18277 | solution.py:100
  103.5 1.3 collective-permute-start.1
  104.8 5.3 %collective-permute-done.1 = f32[1,64]{1,0:T(1,128)S(1)} collective-permute-done((f32[1,64]{1,0:T(1,128)S(1)}, f32[1,64]{1,0:T(1,128)S(1)}, u32[]{:S(2)}, u32[]{:S(2)}) %collective-permute-start.1) | collective-permute-done | bytes 288 | tf_op jit(solution)/shard_map/while/body/eval_jaxpr/ppermute | solution.py:12
  110.2 1.3 collective-permute-start.1
  111.5 5.3 %collective-permute-done.1 = f32[1,64]{1,0:T(1,128)S(1)} collective-permute-done((f32[1,64]{1,0:T(1,128)S(1)}, f32[1,64]{1,0:T(1,128)S(1)}, u32[]{:S(2)}, u32[]{:S(2)}) %collective-permute-start.1) | collective-permute-done | bytes 288 | tf_op jit(solution)/shard_map/while/body/eval_jaxpr/ppermute | solution.py:12
  116.9 1.3 collective-permute-start.1
  118.2 5.0 %collective-permute-done.1 = f32[1,64]{1,0:T(1,128)S(1)} collective-permute-done((f32[1,64]{1,0:T(1,128)S(1)}, f32[1,64]{1,0:T(1,128)S(1)}, u32[]{:S(2)}, u32[]{:S(2)}) %collective-permute-start.1) | collective-permute-done | bytes 288 | tf_op jit(solution)/shard_map/while/body/eval_jaxpr/ppermute | solution.py:12
  123.4 1.3 collective-permute-start.1
  124.7 5.0 %collective-permute-done.1 = f32[1,64]{1,0:T(1,128)S(1)} collective-permute-done((f32[1,64]{1,0:T(1,128)S(1)}, f32[1,64]{1,0:T(1,128)S(1)}, u32[]{:S(2)}, u32[]{:S(2)}) %collective-permute-start.1) | collective-permute-done | bytes 288 | tf_op jit(solution)/shard_map/while/body/eval_jaxpr/ppermute | solution.py:12
  129.9 1.3 collective-permute-start.1
  131.2 5.0 %collective-permute-done.1 = f32[1,64]{1,0:T(1,128)S(1)} collective-permute-done((f32[1,64]{1,0:T(1,128)S(1)}, f32[1,64]{1,0:T(1,128)S(1)}, u32[]{:S(2)}, u32[]{:S(2)}) %collective-permute-start.1) | collective-permute-done | bytes 288 | tf_op jit(solution)/shard_map/while/body/eval_jaxpr/ppermute | solution.py:12
  136.4 1.3 collective-permute-start.1
  137.7 5.0 %collective-permute-done.1 = f32[1,64]{1,0:T(1,128)S(1)} collective-permute-done((f32[1,64]{1,0:T(1,128)S(1)}, f32[1,64]{1,0:T(1,128)S(1)}, u32[]{:S(2)}, u32[]{:S(2)}) %collective-permute-start.1) | collective-permute-done | bytes 288 | tf_op jit(solution)/shard_map/while/body/eval_jaxpr/ppermute | solution.py:12
  142.9 1.3 collective-permute-start.1
  144.2 5.0 %collective-permute-done.1 = f32[1,64]{1,0:T(1,128)S(1)} collective-permute-done((f32[1,64]{1,0:T(1,128)S(1)}, f32[1,64]{1,0:T(1,128)S(1)}, u32[]{:S(2)}, u32[]{:S(2)}) %collective-permute-start.1) | collective-permute-done | bytes 288 | tf_op jit(solution)/shard_map/while/body/eval_jaxpr/ppermute | solution.py:12
  149.3 2.5 %fusion.59 = f32[1,32,64]{2,0,1:T(1,128)S(1)} fusion(f32[32,64,64]{2,1,0:T(8,128)S(1)} %copy-done.13, f32[1,64]{1,0:T(1,128)S(1)} %get-tuple-element.50), kind=kOutput, calls=%fused_computation.96 | convolution fusion | flops 1572864 | bytes 532736 | tf_op jit(solution)/shard_map/...ij,...j->...i/dot_general | solution.py:24
  (135 shorter events, 6.9 us)
Async XLA Ops:
  0.7 35.0 %collective-permute-start.3 = (f32[1,1,64]{2,1,0:T(1,128)S(1)}, f32[1,1,64]{2,1,0:T(1,128)S(1)}, u32[]{:S(2)}, u32[]{:S(2)}) collective-permute-start(f32[1,1,64]{2,1,0:T(1,128)S(1)} %slice.96), channel_id=1, source_target_pairs={{4,0},{8,4},{12,8},{16,12},{20,16},{24,20},{28,24},{5,1},{9,5},{13... | collective-permute-start | bytes 776 | tf_op jit(solution)/shard_map/ppermute | solution.py:12
  2.7 5.5 %copy-start.20 = (f32[1,32,64]{2,1,0:T(8,128)S(1)}, f32[1,32,64]{2,1,0:T(8,128)}, u32[]{:S(2)}) copy-start(f32[1,32,64]{2,1,0:T(8,128)} %param.13) | copy-start | bytes 24580
  2.7 32.9 %collective-permute-start.2 = (f32[1,1,64]{2,1,0:T(1,128)S(1)}, f32[1,1,64]{2,1,0:T(1,128)S(1)}, u32[]{:S(2)}, u32[]{:S(2)}) collective-permute-start(f32[1,1,64]{2,1,0:T(1,128)S(1)} %slice.125), channel_id=1, source_target_pairs={{0,4},{4,8},{8,12},{12,16},{16,20},{20,24},{24,28},{1,5},{5,9},{9,... | collective-permute-start | bytes 776 | tf_op jit(solution)/shard_map/ppermute | solution.py:12
  13.5 1.5 %copy-start.17 = (f32[1,32,4096]{2,1,0:T(8,128)S(1)}, f32[1,32,4096]{2,1,0:T(8,128)}, u32[]{:S(2)}) copy-start(f32[1,32,4096]{2,1,0:T(8,128)} %param.20) | copy-start | bytes 1572868
  15.1 0.7 copy-start.25
  15.1 2.3 %copy-start.19 = (f32[1,32,4096]{2,1,0:T(8,128)S(1)}, f32[1,32,4096]{2,1,0:T(8,128)}, u32[]{:S(2)}) copy-start(f32[1,32,4096]{2,1,0:T(8,128)} %param.15) | copy-start | bytes 1572868
  15.7 0.7 copy-start.24
  16.7 0.7 copy-start.18
  23.0 1.3 copy-start.2
  24.3 1.3 copy-start.6
  25.6 1.3 copy-start.10
  26.9 1.3 copy-start.14
  28.2 1.5 copy-start
  29.7 1.3 copy-start.4
  31.0 1.3 copy-start.8
  31.1 2.2 %copy-start.16 = (f32[32,64,64]{2,1,0:T(8,128)S(1)}, f32[32,64,64]{2,1,0:T(8,128)}, u32[]{:S(2)}) copy-start(f32[32,64,64]{2,1,0:T(8,128)} %reshape.284) | copy-start | bytes 1572868
  32.3 1.0 copy-start.12
  35.6 0.7 copy-start.21
  35.6 0.7 copy-start.22
  35.6 0.7 copy-start.23
  38.1 3.6 %copy-start.3 = (f32[32,64,64]{2,1,0:T(8,128)S(1)}, f32[32,64,64]{2,1,0:T(8,128)}, u32[]{:S(2)}) copy-start(f32[32,64,64]{2,1,0:T(8,128)} %copy-done.2) | copy-start | bytes 1572868
  40.0 3.6 %copy-start.7 = (f32[32,64,64]{2,1,0:T(8,128)S(1)}, f32[32,64,64]{2,1,0:T(8,128)}, u32[]{:S(2)}) copy-start(f32[32,64,64]{2,1,0:T(8,128)} %copy-done.6) | copy-start | bytes 1572868
  41.8 3.6 %copy-start.11 = (f32[32,64,64]{2,1,0:T(8,128)S(1)}, f32[32,64,64]{2,1,0:T(8,128)}, u32[]{:S(2)}) copy-start(f32[32,64,64]{2,1,0:T(8,128)} %copy-done.10) | copy-start | bytes 1572868
  43.6 46.5 %copy-start.15 = (f32[32,64,64]{2,1,0:T(8,128)S(1)}, f32[32,64,64]{2,1,0:T(8,128)}, u32[]{:S(2)}) copy-start(f32[32,64,64]{2,1,0:T(8,128)} %copy-done.14) | copy-start | bytes 1572868
  47.5 6.1 %collective-permute-start = (f32[1,64]{1,0:T(1,128)S(1)}, f32[1,64]{1,0:T(1,128)S(1)}, u32[]{:S(2)}, u32[]{:S(2)}) collective-permute-start(f32[1,64]{1,0:T(1,128)S(1)} %fusion.125), channel_id=1, source_target_pairs={{0,4},{4,8},{8,12},{12,16},{16,20},{20,24},{24,28},{1,5},{5,9},{9,... | collective-permute-start | bytes 776 | tf_op jit(solution)/shard_map/while/body/eval_jaxpr/ppermute | solution.py:12
  53.7 5.5 %collective-permute-start = (f32[1,64]{1,0:T(1,128)S(1)}, f32[1,64]{1,0:T(1,128)S(1)}, u32[]{:S(2)}, u32[]{:S(2)}) collective-permute-start(f32[1,64]{1,0:T(1,128)S(1)} %fusion.125), channel_id=1, source_target_pairs={{0,4},{4,8},{8,12},{12,16},{16,20},{20,24},{24,28},{1,5},{5,9},{9,... | collective-permute-start | bytes 776 | tf_op jit(solution)/shard_map/while/body/eval_jaxpr/ppermute | solution.py:12
  59.3 5.5 %collective-permute-start = (f32[1,64]{1,0:T(1,128)S(1)}, f32[1,64]{1,0:T(1,128)S(1)}, u32[]{:S(2)}, u32[]{:S(2)}) collective-permute-start(f32[1,64]{1,0:T(1,128)S(1)} %fusion.125), channel_id=1, source_target_pairs={{0,4},{4,8},{8,12},{12,16},{16,20},{20,24},{24,28},{1,5},{5,9},{9,... | collective-permute-start | bytes 776 | tf_op jit(solution)/shard_map/while/body/eval_jaxpr/ppermute | solution.py:12
  64.9 5.6 %collective-permute-start = (f32[1,64]{1,0:T(1,128)S(1)}, f32[1,64]{1,0:T(1,128)S(1)}, u32[]{:S(2)}, u32[]{:S(2)}) collective-permute-start(f32[1,64]{1,0:T(1,128)S(1)} %fusion.125), channel_id=1, source_target_pairs={{0,4},{4,8},{8,12},{12,16},{16,20},{20,24},{24,28},{1,5},{5,9},{9,... | collective-permute-start | bytes 776 | tf_op jit(solution)/shard_map/while/body/eval_jaxpr/ppermute | solution.py:12
  70.7 6.4 %collective-permute-start = (f32[1,64]{1,0:T(1,128)S(1)}, f32[1,64]{1,0:T(1,128)S(1)}, u32[]{:S(2)}, u32[]{:S(2)}) collective-permute-start(f32[1,64]{1,0:T(1,128)S(1)} %fusion.125), channel_id=1, source_target_pairs={{0,4},{4,8},{8,12},{12,16},{16,20},{20,24},{24,28},{1,5},{5,9},{9,... | collective-permute-start | bytes 776 | tf_op jit(solution)/shard_map/while/body/eval_jaxpr/ppermute | solution.py:12
  77.2 6.4 %collective-permute-start = (f32[1,64]{1,0:T(1,128)S(1)}, f32[1,64]{1,0:T(1,128)S(1)}, u32[]{:S(2)}, u32[]{:S(2)}) collective-permute-start(f32[1,64]{1,0:T(1,128)S(1)} %fusion.125), channel_id=1, source_target_pairs={{0,4},{4,8},{8,12},{12,16},{16,20},{20,24},{24,28},{1,5},{5,9},{9,... | collective-permute-start | bytes 776 | tf_op jit(solution)/shard_map/while/body/eval_jaxpr/ppermute | solution.py:12
  83.7 6.4 %collective-permute-start = (f32[1,64]{1,0:T(1,128)S(1)}, f32[1,64]{1,0:T(1,128)S(1)}, u32[]{:S(2)}, u32[]{:S(2)}) collective-permute-start(f32[1,64]{1,0:T(1,128)S(1)} %fusion.125), channel_id=1, source_target_pairs={{0,4},{4,8},{8,12},{12,16},{16,20},{20,24},{24,28},{1,5},{5,9},{9,... | collective-permute-start | bytes 776 | tf_op jit(solution)/shard_map/while/body/eval_jaxpr/ppermute | solution.py:12
  94.4 3.6 %copy-start.1 = (f32[32,64,64]{2,1,0:T(8,128)S(1)}, f32[32,64,64]{2,1,0:T(8,128)}, u32[]{:S(2)}) copy-start(f32[32,64,64]{2,1,0:T(8,128)} %copy-done) | copy-start | bytes 1572868
  96.2 3.6 %copy-start.5 = (f32[32,64,64]{2,1,0:T(8,128)S(1)}, f32[32,64,64]{2,1,0:T(8,128)}, u32[]{:S(2)}) copy-start(f32[32,64,64]{2,1,0:T(8,128)} %copy-done.4) | copy-start | bytes 1572868
  98.0 3.6 %copy-start.9 = (f32[32,64,64]{2,1,0:T(8,128)S(1)}, f32[32,64,64]{2,1,0:T(8,128)}, u32[]{:S(2)}) copy-start(f32[32,64,64]{2,1,0:T(8,128)} %copy-done.8) | copy-start | bytes 1572868
  99.8 49.5 %copy-start.13 = (f32[32,64,64]{2,1,0:T(8,128)S(1)}, f32[32,64,64]{2,1,0:T(8,128)}, u32[]{:S(2)}) copy-start(f32[32,64,64]{2,1,0:T(8,128)} %copy-done.12) | copy-start | bytes 1572868
  103.5 6.6 %collective-permute-start.1 = (f32[1,64]{1,0:T(1,128)S(1)}, f32[1,64]{1,0:T(1,128)S(1)}, u32[]{:S(2)}, u32[]{:S(2)}) collective-permute-start(f32[1,64]{1,0:T(1,128)S(1)} %fusion.128), channel_id=1, source_target_pairs={{4,0},{8,4},{12,8},{16,12},{20,16},{24,20},{28,24},{5,1},{9,5},{13... | collective-permute-start | bytes 776 | tf_op jit(solution)/shard_map/while/body/eval_jaxpr/ppermute | solution.py:12
  110.2 6.6 %collective-permute-start.1 = (f32[1,64]{1,0:T(1,128)S(1)}, f32[1,64]{1,0:T(1,128)S(1)}, u32[]{:S(2)}, u32[]{:S(2)}) collective-permute-start(f32[1,64]{1,0:T(1,128)S(1)} %fusion.128), channel_id=1, source_target_pairs={{4,0},{8,4},{12,8},{16,12},{20,16},{24,20},{28,24},{5,1},{9,5},{13... | collective-permute-start | bytes 776 | tf_op jit(solution)/shard_map/while/body/eval_jaxpr/ppermute | solution.py:12
  116.9 6.4 %collective-permute-start.1 = (f32[1,64]{1,0:T(1,128)S(1)}, f32[1,64]{1,0:T(1,128)S(1)}, u32[]{:S(2)}, u32[]{:S(2)}) collective-permute-start(f32[1,64]{1,0:T(1,128)S(1)} %fusion.128), channel_id=1, source_target_pairs={{4,0},{8,4},{12,8},{16,12},{20,16},{24,20},{28,24},{5,1},{9,5},{13... | collective-permute-start | bytes 776 | tf_op jit(solution)/shard_map/while/body/eval_jaxpr/ppermute | solution.py:12
  123.4 6.4 %collective-permute-start.1 = (f32[1,64]{1,0:T(1,128)S(1)}, f32[1,64]{1,0:T(1,128)S(1)}, u32[]{:S(2)}, u32[]{:S(2)}) collective-permute-start(f32[1,64]{1,0:T(1,128)S(1)} %fusion.128), channel_id=1, source_target_pairs={{4,0},{8,4},{12,8},{16,12},{20,16},{24,20},{28,24},{5,1},{9,5},{13... | collective-permute-start | bytes 776 | tf_op jit(solution)/shard_map/while/body/eval_jaxpr/ppermute | solution.py:12
  129.9 6.4 %collective-permute-start.1 = (f32[1,64]{1,0:T(1,128)S(1)}, f32[1,64]{1,0:T(1,128)S(1)}, u32[]{:S(2)}, u32[]{:S(2)}) collective-permute-start(f32[1,64]{1,0:T(1,128)S(1)} %fusion.128), channel_id=1, source_target_pairs={{4,0},{8,4},{12,8},{16,12},{20,16},{24,20},{28,24},{5,1},{9,5},{13... | collective-permute-start | bytes 776 | tf_op jit(solution)/shard_map/while/body/eval_jaxpr/ppermute | solution.py:12
  136.4 6.4 %collective-permute-start.1 = (f32[1,64]{1,0:T(1,128)S(1)}, f32[1,64]{1,0:T(1,128)S(1)}, u32[]{:S(2)}, u32[]{:S(2)}) collective-permute-start(f32[1,64]{1,0:T(1,128)S(1)} %fusion.128), channel_id=1, source_target_pairs={{4,0},{8,4},{12,8},{16,12},{20,16},{24,20},{28,24},{5,1},{9,5},{13... | collective-permute-start | bytes 776 | tf_op jit(solution)/shard_map/while/body/eval_jaxpr/ppermute | solution.py:12
  142.9 6.4 %collective-permute-start.1 = (f32[1,64]{1,0:T(1,128)S(1)}, f32[1,64]{1,0:T(1,128)S(1)}, u32[]{:S(2)}, u32[]{:S(2)}) collective-permute-start(f32[1,64]{1,0:T(1,128)S(1)} %fusion.128), channel_id=1, source_target_pairs={{4,0},{8,4},{12,8},{16,12},{20,16},{24,20},{28,24},{5,1},{9,5},{13... | collective-permute-start | bytes 776 | tf_op jit(solution)/shard_map/while/body/eval_jaxpr/ppermute | solution.py:12
where the time goes:
time: 153 us; the launch traced here: 152 us
  starting transfers between devices  48.7 us (32%)
  waiting for transfers between devices  44.6 us (29%)
  matrix products  41.8 us (27%)
  local copies, waits for them, and re-layouts  9.01 us (6%)
  blocking collectives  5.25 us (3%)
  other arithmetic  1.92 us (1%)
    ppermute x16, starting transfers between devices, passed_along(): lax.ppermute(value, axis, [(source, source + steps) for source in range(f...  48.7 us
    ppermute x16, waiting for transfers between devices, passed_along(): lax.ppermute(value, axis, [(source, source + steps) for source in range(f...  44.6 us
    dot_general x10, matrix products, compose(): jnp.einsum('...ij,...j->...i', last_mat, first_vec, precision=highest)  17.4 us
    dot_general x10, matrix products, compose(): jnp.einsum('...ij,...jk->...ik', last_mat, first_mat, precision=highest)  12.1 us
    dot_general x18, matrix products, apply_map(): return jnp.einsum('...ij,...j->...i', matrix, vector, precision=highest)  10.6 us
    all_gather x1, blocking collectives, on_device(): all_lines = lax.all_gather(densities, 'lat', axis=0, tiled=True)  5.25 us
    unnamed x52, local copies, waits for them, and re-layouts  3.28 us
  transfers between devices with their start and end apart: 16, of which 14 were waited for; matrix products, arithmetic and copies ran while one was open for 13% of the time, Pallas kernels for 0%

commit v1 on v0

v1 whole, which is shorter than its diff:
```python
import functools

import jax
import jax.numpy as jnp
from jax import lax
from jax.experimental import pallas as pl
from jax.experimental.pallas import tpu as pltpu
from jax.sharding import PartitionSpec as P

MESH = pl.DeviceIdType.MESH
F32 = jnp.float32
BF16 = jnp.bfloat16
ROWS = 8


def split(x):
    high = x.astype(BF16)
    return high, (x - high.astype(F32)).astype(BF16)


def part(pair, index):
    return pair[0][index], pair[1][index]


def dot3(a, b, dims):
    def one(x, y):
        return lax.dot_general(x, y, dims, preferred_element_type=F32)

    return one(a[0], b[0]) + (one(a[0], b[1]) + one(a[1], b[0]))


def widen(x):
    return jnp.concatenate([x, jnp.zeros_like(x)], axis=x.ndim - 1)


def mats(a, b):
    return dot3(tuple(x[:, :, : x.shape[1]] for x in a), b, (((2,), (1,)), ((0,), (0,))))


def vecs(a, v):
    return dot3(split(widen(v)), a, (((2,), (2,)), ((0,), (0,))))


def row_times(v, a):
    return dot3(split(widen(v)), a, (((1,), (1,)), ((), ())))


def pack(x):
    half = x.shape[0] // 2
    return jnp.concatenate([x[:half], x[half:]], axis=1)


def unpack(x):
    half = x.shape[1] // 2
    return jnp.concatenate([x[:, :half], x[:, half:]], axis=0)


def pairs(x):
    y = x.reshape((x.shape[0] // 2, 2) + x.shape[1:])
    return y[:, 0], y[:, 1]


def pair_up(even, odd):
    y = jnp.stack([even, odd], axis=1)
    return y.reshape((2 * even.shape[0],) + even.shape[1:])


def kernel(
    depth_count,
    lat_count,
    dens_ref,
    source_ref,
    jac_hbm,
    pattern_ref,
    transport_ref,
    lateral_ref,
    neighbours_ref,
    factor_hbm,
    coupling_ref,
    out_ref,
    jac_ref,
    factor_ref,
    inv_ref,
    vec_ref,
    lines_ref,
    row_out,
    row_in,
    mat_out,
    fwd_mats,
    bwd_mats,
    vec_out,
    fwd_vecs,
    bwd_vecs,
    load_sem,
    line_send,
    line_recv,
    row_send,
    row_recv,
    mat_send,
    fwd_mat_recv,
    bwd_mat_recv,
    fwd_send,
    fwd_recv,
    bwd_send,
    bwd_recv,
):
    d = lax.axis_index("depth")
    line = lax.axis_index("lat")
    cells, species = dens_ref.shape[1:]
    width = 2 * species
    chunks = species // 2
    last = depth_count - 1

    load_factor = pltpu.make_async_copy(factor_hbm, factor_ref, load_sem.at[0])
    load_jac = pltpu.make_async_copy(jac_hbm, jac_ref, load_sem.at[1])
    load_factor.start()
    load_jac.start()

    barrier = pltpu.get_barrier_semaphore()

    def greet_depth(e, carry):
        @pl.when(e != d)
        def _():
            pl.semaphore_signal(barrier, inc=1, device_id={"depth": e}, device_id_type=MESH)

        return carry

    def greet_lat(e, carry):
        @pl.when(e != line)
        def _():
            pl.semaphore_signal(barrier, inc=1, device_id={"lat": e}, device_id_type=MESH)

        return carry

    lax.fori_loop(0, depth_count, greet_depth, 0)
    lax.fori_loop(0, lat_count, greet_lat, 0)
    dens = dens_ref[0]
    transport = transport_ref[0]
    coupling = coupling_ref[0]
    flux = transport * dens
    row_out[0] = flux[cells - 1 :, :]
    row_out[1] = dens[:1, :]
    lines_ref[line] = dens
    pl.semaphore_wait(barrier, depth_count + lat_count - 2)

    def line_copy(source, target):
        return pltpu.make_async_remote_copy(
            src_ref=dens_ref.at[0],
            dst_ref=lines_ref.at[source],
            send_sem=line_send.at[target],
            recv_sem=line_recv.at[source],
            device_id={"lat": target},
            device_id_type=MESH,
        )

    def row_copy(which, target):
        return pltpu.make_async_remote_copy(
            src_ref=row_out.at[which],
            dst_ref=row_in.at[which],
            send_sem=row_send.at[which],
            recv_sem=row_recv.at[which],
            device_id={"depth": target},
            device_id_type=MESH,
        )

    def mat_copy(which, source, target):
        return pltpu.make_async_remote_copy(
            src_ref=mat_out.at[which],
            dst_ref=(fwd_mats, bwd_mats)[which].at[source],
            send_sem=mat_send.at[target],
            recv_sem=(fwd_mat_recv, bwd_mat_recv)[which].at[source],
            device_id={"depth": target},
            device_id_type=MESH,
        )

    def vec_copy(which, source, target):
        return pltpu.make_async_remote_copy(
            src_ref=vec_out.at[which],
            dst_ref=(fwd_vecs, bwd_vecs)[which].at[source],
            send_sem=(fwd_send, bwd_send)[which].at[target],
            recv_sem=(fwd_recv, bwd_recv)[which].at[source],
            device_id={"depth": target},
            device_id_type=MESH,
        )

    def each_line(act):
        def body(e, carry):
            @pl.when(e != line)
            def _():
                act(e)

            return carry

        lax.fori_loop(0, lat_count, body, 0)

    def each_later(act):
        def body(e, carry):
            act(e)
            return carry

        lax.fori_loop(d + 1, depth_count, body, 0)

    def each_earlier(act):
        def body(i, carry):
            act(d - 1 - i)
            return carry

        lax.fori_loop(0, d, body, 0)

    each_line(lambda e: line_copy(line, e).start())

    @pl.when(d < last)
    def _():
        row_copy(0, d + 1).start()

    @pl.when(d > 0)
    def _():
        row_copy(1, d - 1).start()

    @pl.when(d == 0)
    def _():
        row_in[0] = jnp.zeros((1, species), F32)

    @pl.when(d == last)
    def _():
        row_in[1] = jnp.zeros((1, species), F32)

    used = [0]

    def settle(values):
        at = used[0]
        used[0] += values.shape[0]
        vec_ref[at : used[0]] = values
        return vec_ref[at : used[0]]

    inv_ref[...] = jnp.zeros_like(inv_ref)
    load_factor.wait()
    for first in range(0, cells, 8):
        for p in range(chunks):
            values = factor_ref[0, first : first + 8, p * width : (p + 1) * width]
            start = first * species + 2 * p
            inv_ref[pl.ds(start, 8, stride=species), :species] = values[:, :species]
            inv_ref[pl.ds(start + 1, 8, stride=species), :species] = values[:, species:]
    inverse = inv_ref[...].reshape(cells, species, width)
    coup = widen(coupling).reshape(cells, 1, width)
    coup_before = jnp.concatenate([jnp.ones((1, 1, width), F32), coup[:-1]], axis=0)
    inv = split(inverse)

    fwd_levels = [split(inverse * coup_before)]
    bwd_levels = [split(inverse * coup)]
    group = cells
    while group > 1:
        group //= 2
        fwd_low, fwd_high = zip(*(pairs(x) for x in fwd_levels[-1]))
        bwd_low, bwd_high = zip(*(pairs(x) for x in bwd_levels[-1]))
        fwd = mats(fwd_high, fwd_low)
        bwd = mats(bwd_low, bwd_high)
        if group > 1:
            fwd_levels.append(split(fwd))
            bwd_levels.append(split(bwd))
    last_coup = coupling[cells - 1 :, :]
    last_column = jnp.broadcast_to(last_coup, (species, species)).T
    mat_out[0] = pack(fwd[0][:, :species] * last_column)
    mat_out[1] = pack(bwd[0][:, :species])
    each_later(lambda e: mat_copy(0, d, e).start())
    each_earlier(lambda e: mat_copy(1, d, e).start())

    tiles = pattern_ref.shape[0]
    tile = species // tiles
    lane = lax.broadcasted_iota(jnp.int32, (tiles, width), 1)
    row = lax.broadcasted_iota(jnp.int32, (tiles, width), 0)
    spread = jnp.where((lane % species) // tile == row, 1.0, 0.0).astype(BF16)
    mask_rows = jnp.dot(
        pattern_ref[...].astype(F32).astype(BF16), spread, preferred_element_type=F32
    )
    dens_twice = jnp.concatenate([dens, dens], axis=1)
    at_row = lax.broadcasted_iota(jnp.int32, (width, species), 0) // species
    at_column = lax.broadcasted_iota(jnp.int32, (width, species), 1)
    offset = at_column - at_row
    load_jac.wait()
    reaction = jnp.zeros((cells, species), F32)
    masked = [mask_rows[t : t + 1] * dens_twice for t in range(tiles)]
    for p in range(chunks):
        terms = split(jac_ref[0, :, p * width : (p + 1) * width] * masked[(2 * p) // tile])
        collect = jnp.where(offset == 2 * p, 1.0, 0.0).astype(BF16)
        reaction += jnp.dot(terms[0], collect, preferred_element_type=F32)
        reaction += jnp.dot(terms[1], collect, preferred_element_type=F32)

    @pl.when(d > 0)
    def _():
        row_copy(0, d).wait_recv()

    @pl.when(d < last)
    def _():
        row_copy(1, d).wait_recv()

    each_line(lambda e: line_copy(e, e).wait_recv())
    near = lines_ref[neighbours_ref[0, 0]]
    for j in range(1, neighbours_ref.shape[1]):
        near += lines_ref[neighbours_ref[0, j]]
    cell = lax.broadcasted_iota(jnp.int32, (cells, species), 0)
    lower_flux = jnp.where(cell == 0, row_in[0], pltpu.roll(flux, 1, 0))
    upper = jnp.where(cell == cells - 1, row_in[1], pltpu.roll(dens, cells - 1, 0))
    operator = (
        reaction - lower_flux - transport * upper + lateral_ref[0] * (4.0 * dens - near)
    )
    residual = source_ref[0] - operator
    pivoted = settle(
        vecs(inv, jnp.broadcast_to(residual.reshape(cells, 1, species), (cells, ROWS, species)))
    )

    heads = []
    carried = pivoted
    for level in fwd_levels:
        low, high = pairs(carried)
        later = tuple(pairs(x)[1] for x in level)
        heads.append(low)
        carried = settle(vecs(later, low) + high)
    vec_out[0] = carried[0][:1] * last_coup
    each_later(lambda e: vec_copy(0, d, e).start())

    def forward_step(e, x):
        mat_copy(0, e, e).wait_recv()
        vec_copy(0, e, e).wait_recv()
        return row_times(x, split(widen(unpack(fwd_mats[e])))) + fwd_vecs[e]

    x = lax.fori_loop(0, d, forward_step, jnp.zeros((ROWS, species), F32))

    entering = x.reshape(1, ROWS, species)
    for level, low in zip(fwd_levels[::-1], heads[::-1]):
        earlier = tuple(pairs(m)[0] for m in level)
        entering = settle(pair_up(entering, vecs(earlier, entering) + low))
    forward_vals = settle(vecs(fwd_levels[0], entering) + pivoted)

    tails = []
    carried = forward_vals
    for level in bwd_levels:
        low, high = pairs(carried)
        earlier = tuple(pairs(m)[0] for m in level)
        tails.append(high)
        carried = settle(low + vecs(earlier, high))
    vec_out[1] = carried[0][:1]
    each_earlier(lambda e: vec_copy(1, d, e).start())

    def backward_step(i, y):
        e = last - i
        mat_copy(1, e, e).wait_recv()
        vec_copy(1, e, e).wait_recv()
        return row_times(y, split(widen(unpack(bwd_mats[e])))) + bwd_vecs[e]

    y = lax.fori_loop(0, last - d, backward_step, jnp.zeros((ROWS, species), F32))
    entering = y.reshape(1, ROWS, species)
    for level, high in zip(bwd_levels[::-1], tails[::-1]):
        later = tuple(pairs(m)[1] for m in level)
        entering = settle(pair_up(vecs(later, entering) + high, entering))
    correction = vecs(bwd_levels[0], entering) + forward_vals
    for k in range(cells):
        out_ref[0, k : k + 1, :] = correction[k][:1]

    each_line(lambda e: line_copy(line, e).wait_send())

    @pl.when(d < last)
    def _():
        row_copy(0, d).wait_send()

    @pl.when(d > 0)
    def _():
        row_copy(1, d).wait_send()

    each_later(lambda e: mat_copy(0, d, e).wait_send())
    each_earlier(lambda e: mat_copy(1, d, e).wait_send())
    each_later(lambda e: vec_copy(0, d, e).wait_send())
    each_earlier(lambda e: vec_copy(1, d, e).wait_send())


def on_device(
    densities, source, jacobian, pattern, transport, lateral, neighbours, factor, coupling
):
    lines, cells, species = densities.shape
    depth_count = lax.axis_size("depth")
    lat_count = lax.axis_size("lat")
    vmem = pl.BlockSpec(memory_space=pltpu.VMEM)
    smem = pl.BlockSpec(memory_space=pltpu.SMEM)
    hbm = pl.BlockSpec(memory_space=pl.ANY)
    dma = pltpu.SemaphoreType.DMA
    return pl.pallas_call(
        functools.partial(kernel, depth_count, lat_count),
        out_shape=jax.ShapeDtypeStruct(densities.shape, F32),
        in_specs=[vmem, vmem, hbm, vmem, vmem, vmem, smem, hbm, vmem],
        out_specs=vmem,
        scratch_shapes=[
            pltpu.VMEM(jacobian.shape, F32),
            pltpu.VMEM(factor.shape, F32),
            pltpu.VMEM((cells * species, 2 * species), F32),
            pltpu.VMEM((8 * cells, ROWS, species), F32),
            pltpu.VMEM((lat_count, cells, species), F32),
            pltpu.VMEM((2, 1, species), F32),
            pltpu.VMEM((2, 1, species), F32),
            pltpu.VMEM((2, species // 2, 2 * species), F32),
            pltpu.VMEM((depth_count, species // 2, 2 * species), F32),
            pltpu.VMEM((depth_count, species // 2, 2 * species), F32),
            pltpu.VMEM((2, 1, species), F32),
            pltpu.VMEM((depth_count, 1, species), F32),
            pltpu.VMEM((depth_count, 1, species), F32),
            dma((2,)),
            dma((lat_count,)),
            dma((lat_count,)),
            dma((2,)),
            dma((2,)),
            dma((depth_count,)),
            dma((depth_count,)),
            dma((depth_count,)),
            dma((depth_count,)),
            dma((depth_count,)),
            dma((depth_count,)),
            dma((depth_count,)),
        ],
        compiler_params=pltpu.CompilerParams(
            collective_id=0, has_side_effects=True, vmem_limit_bytes=48 * 1024 * 1024
        ),
    )(densities, source, jacobian, pattern, transport, lateral, neighbours, factor, coupling)


def solution(mesh):
    return jax.shard_map(
        on_device,
        mesh=mesh,
        in_specs=(
            P("lat", "depth", None),
            P("lat", "depth", None),
            P("lat", "depth", None),
            P(),
            P("lat", "depth", None),
            P("lat", "depth", None),
            P("lat", None),
            P("lat", "depth", None),
            P("lat", "depth", None),
        ),
        out_specs=P("lat", "depth", None),
        check_vma=False,
    )
```

time: 153 us -> 38.4 us (0.25)
  starting transfers between devices: 48.7 us -> 0 us
  waiting for transfers between devices: 44.6 us -> 0 us
  matrix products: 41.8 us -> 0 us
  Pallas kernels: 0 us -> 30.1 us
  blocking collectives: 5.25 us -> 0 us
  other arithmetic: 1.92 us -> 0 us
    ppermute x16 -> x0, starting transfers between devices: 48.7 us -> none  [passed_along(): lax.ppermute(value, axis, [(source, source + steps) for source in range(f...]
    ppermute x16 -> x0, waiting for transfers between devices: 44.6 us -> none  [passed_along(): lax.ppermute(value, axis, [(source, source + steps) for source in range(f...]
    dot_general x39 -> x0, matrix products: 41.8 us -> none  [the longest x10 17.4 us: compose(): jnp.einsum('...ij,...j->...i', last_mat, first_vec, precision=highest)]
    pallas_call x0 -> x1, Pallas kernels: none -> 30.1 us  [on_device(): pl.pallas_call(functools.partial(kernel, depth_count, lat_count), out_sha...]
    all_gather x1 -> x0, blocking collectives: 5.25 us -> none  [on_device(): all_lines = lax.all_gather(densities, 'lat', axis=0, tiled=True)]
    unnamed x52 -> x19, local copies, waits for them, and re-layouts: 3.28 us -> 7.62 us
    reshape x7 -> x0, local copies, waits for them, and re-layouts: 3.47 us -> none  [the longest x2 1.93 us: on_device(): inverses = factor.reshape(line_count, cell_count, species, species)]
  transfers between devices with their start and end apart: 16 -> 0, of which waited for: 14 -> 0; matrix products, arithmetic and copies ran while one was open for 13% -> 0% of each run, Pallas kernels for 0% -> 0%
where the time goes in v1:
time: 38.4 us; the launch traced here: 37.7 us
  Pallas kernels  30.1 us (78%)
  local copies, waits for them, and re-layouts  7.62 us (20%)
    pallas_call x1, Pallas kernels, on_device(): pl.pallas_call(functools.partial(kernel, depth_count, lat_count), out_sha...  30.1 us
    unnamed x19, local copies, waits for them, and re-layouts  7.62 us

profile of v1, /device:TPU:0, one launch (start us, length us, event | category | flops | bytes accessed | tf_op | source)
XLA Modules:
  0.0 37.7 jit_solution(9534781955253367898)
XLA Ops:
  0.0 0.0 copy-start
  0.0 1.0 %copy-done = f32[1,32,4096]{2,1,0:T(8,128)S(1)} copy-done((f32[1,32,4096]{2,1,0:T(8,128)S(1)}, f32[1,32,4096]{2,1,0:T(8,128)}, u32[]{:S(2)}) %copy-start) | copy-done | bytes 524312
  1.0 0.0 copy-start.1
  1.0 1.0 %copy-done.1 = f32[1,32,4096]{2,1,0:T(8,128)S(1)} copy-done((f32[1,32,4096]{2,1,0:T(8,128)S(1)}, f32[1,32,4096]{2,1,0:T(8,128)}, u32[]{:S(2)}) %copy-start.1) | copy-done | bytes 524312
  2.1 0.0 copy-start.2
  2.1 0.7 %copy-done.2 = f32[1,32,64]{2,1,0:T(8,128)S(1)} copy-done((f32[1,32,64]{2,1,0:T(8,128)S(1)}, f32[1,32,64]{2,1,0:T(8,128)}, u32[]{:S(2)}) %copy-start.2) | copy-done | bytes 8216
  2.8 0.0 copy-start.3
  2.8 0.7 %copy-done.3 = f32[1,32,64]{2,1,0:T(8,128)S(1)} copy-done((f32[1,32,64]{2,1,0:T(8,128)S(1)}, f32[1,32,64]{2,1,0:T(8,128)}, u32[]{:S(2)}) %copy-start.3) | copy-done | bytes 8216
  3.5 0.0 copy-start.4
  3.5 0.7 %copy-done.4 = f32[1,32,64]{2,1,0:T(8,128)S(1)} copy-done((f32[1,32,64]{2,1,0:T(8,128)S(1)}, f32[1,32,64]{2,1,0:T(8,128)}, u32[]{:S(2)}) %copy-start.4) | copy-done | bytes 8216
  4.2 0.0 copy-start.5
  4.2 0.7 %copy-done.5 = f32[1,32,64]{2,1,0:T(8,128)S(1)} copy-done((f32[1,32,64]{2,1,0:T(8,128)S(1)}, f32[1,32,64]{2,1,0:T(8,128)}, u32[]{:S(2)}) %copy-start.5) | copy-done | bytes 8216
  5.0 0.0 copy-start.6
  5.0 0.7 %copy-done.6 = f32[1,32,64]{2,1,0:T(8,128)S(1)} copy-done((f32[1,32,64]{2,1,0:T(8,128)S(1)}, f32[1,32,64]{2,1,0:T(8,128)}, u32[]{:S(2)}) %copy-start.6) | copy-done | bytes 8216
  5.7 0.0 copy-start.7
  5.7 0.7 %copy-done.7 = s32[8,8]{1,0:T(8,128)S(1)} copy-done((s32[8,8]{1,0:T(8,128)S(1)}, s32[8,8]{1,0:T(8,128)}, u32[]{:S(2)}) %copy-start.7) | copy-done | bytes 280
  6.4 0.0 copy-start.8
  6.4 0.7 %copy-done.8 = s32[1,4]{1,0:T(1,128)S(1)} copy-done((s32[1,4]{1,0:T(1,128)S(1)}, s32[1,4]{1,0:T(1,128)}, u32[]{:S(2)}) %copy-start.8) | copy-done | bytes 40
  7.0 30.1 %shard_map.91 = f32[1,32,64]{2,1,0:T(8,128)S(1)} custom-call(f32[1,32,64]{2,1,0:T(8,128)S(1)} %copy-done.2, f32[1,32,64]{2,1,0:T(8,128)S(1)} %copy-done.3, f32[1,32,4096]{2,1,0:T(8,128)S(1)} %copy-done, s32[8,8]{1,0:T(8,128)S(1)} %copy-done.7, f32[1,32,64]{2,1,0:T(8,128)S(1)} %copy-done.4, f32[1,32,64]{2,1,0:T(8,128)S(1)} %copy-done.5, ...), custom_call_target="tpu_custom_call" | custom-call | tf_op jit(solution)/shard_map/pallas_call | solution.py:386
  37.1 0.6 %copy.11 = f32[1,32,64]{2,1,0:T(8,128)} copy(f32[1,32,64]{2,1,0:T(8,128)S(1)} %shard_map.91) | data formatting | bytes 16384
Async XLA Ops:
  0.0 1.0 %copy-start = (f32[1,32,4096]{2,1,0:T(8,128)S(1)}, f32[1,32,4096]{2,1,0:T(8,128)}, u32[]{:S(2)}) copy-start(f32[1,32,4096]{2,1,0:T(8,128)} %jac_hbm.1) | copy-start | bytes 1572868
  1.0 1.0 %copy-start.1 = (f32[1,32,4096]{2,1,0:T(8,128)S(1)}, f32[1,32,4096]{2,1,0:T(8,128)}, u32[]{:S(2)}) copy-start(f32[1,32,4096]{2,1,0:T(8,128)} %factor_hbm.1) | copy-start | bytes 1572868
  2.1 0.7 %copy-start.2 = (f32[1,32,64]{2,1,0:T(8,128)S(1)}, f32[1,32,64]{2,1,0:T(8,128)}, u32[]{:S(2)}) copy-start(f32[1,32,64]{2,1,0:T(8,128)} %dens_ref.1) | copy-start | bytes 24580
  2.8 0.7 %copy-start.3 = (f32[1,32,64]{2,1,0:T(8,128)S(1)}, f32[1,32,64]{2,1,0:T(8,128)}, u32[]{:S(2)}) copy-start(f32[1,32,64]{2,1,0:T(8,128)} %source_ref.1) | copy-start | bytes 24580
  3.5 0.7 %copy-start.4 = (f32[1,32,64]{2,1,0:T(8,128)S(1)}, f32[1,32,64]{2,1,0:T(8,128)}, u32[]{:S(2)}) copy-start(f32[1,32,64]{2,1,0:T(8,128)} %transport_ref.1) | copy-start | bytes 24580
  4.2 0.7 %copy-start.5 = (f32[1,32,64]{2,1,0:T(8,128)S(1)}, f32[1,32,64]{2,1,0:T(8,128)}, u32[]{:S(2)}) copy-start(f32[1,32,64]{2,1,0:T(8,128)} %lateral_ref.1) | copy-start | bytes 24580
  5.0 0.7 %copy-start.6 = (f32[1,32,64]{2,1,0:T(8,128)S(1)}, f32[1,32,64]{2,1,0:T(8,128)}, u32[]{:S(2)}) copy-start(f32[1,32,64]{2,1,0:T(8,128)} %coupling_ref.1) | copy-start | bytes 24580
  5.7 0.7 %copy-start.7 = (s32[8,8]{1,0:T(8,128)S(1)}, s32[8,8]{1,0:T(8,128)}, u32[]{:S(2)}) copy-start(s32[8,8]{1,0:T(8,128)} %pattern_ref.1) | copy-start | bytes 772
  6.4 0.7 %copy-start.8 = (s32[1,4]{1,0:T(1,128)S(1)}, s32[1,4]{1,0:T(1,128)}, u32[]{:S(2)}) copy-start(s32[1,4]{1,0:T(1,128)} %neighbours_ref.1) | copy-start | bytes 52

commit v2 on v1

--- a/solution.py
+++ b/solution.py
@@ -37,12 +37,22 @@
     return dot3(tuple(x[:, :, : x.shape[1]] for x in a), b, (((2,), (1,)), ((0,), (0,))))
 
 
+def dot_rows(v, a, dims):
+    rows = v.ndim - 2
+    wide = widen(v)
+    high = wide.astype(BF16).astype(F32)
+    both = jnp.concatenate([high, wide - high], axis=rows).astype(BF16)
+    total = lax.dot_general(both, a[0], dims, preferred_element_type=F32)
+    total += lax.dot_general(both, a[1], dims, preferred_element_type=F32)
+    return total[..., :ROWS, :] + total[..., ROWS:, :]
+
+
 def vecs(a, v):
-    return dot3(split(widen(v)), a, (((2,), (2,)), ((0,), (0,))))
+    return dot_rows(v, a, (((2,), (2,)), ((0,), (0,))))
 
 
 def row_times(v, a):
-    return dot3(split(widen(v)), a, (((1,), (1,)), ((), ())))
+    return dot_rows(v, a, (((1,), (1,)), ((), ())))
 
 
 def pack(x):

time: 38.4 us -> 36.1 us (0.940)
  Pallas kernels: 30.1 us -> 27.8 us
    pallas_call x1, Pallas kernels: 30.1 us -> 27.8 us  [on_device(): pl.pallas_call(functools.partial(kernel, depth_count, lat_count), out_sha...]
where the time goes in v2:
time: 36.1 us; the launch traced here: 35.4 us
  Pallas kernels  27.8 us (77%)
  local copies, waits for them, and re-layouts  7.62 us (21%)
    pallas_call x1, Pallas kernels, on_device(): pl.pallas_call(functools.partial(kernel, depth_count, lat_count), out_sha...  27.8 us
    unnamed x19, local copies, waits for them, and re-layouts  7.62 us

profile of v2, /device:TPU:0, one launch (start us, length us, event | category | flops | bytes accessed | tf_op | source)
XLA Modules:
  0.0 35.4 jit_solution(7706329709222868844)
XLA Ops:
  0.0 0.0 copy-start
  0.0 1.0 %copy-done = f32[1,32,4096]{2,1,0:T(8,128)S(1)} copy-done((f32[1,32,4096]{2,1,0:T(8,128)S(1)}, f32[1,32,4096]{2,1,0:T(8,128)}, u32[]{:S(2)}) %copy-start) | copy-done | bytes 524312
  1.0 0.0 copy-start.1
  1.0 1.0 %copy-done.1 = f32[1,32,4096]{2,1,0:T(8,128)S(1)} copy-done((f32[1,32,4096]{2,1,0:T(8,128)S(1)}, f32[1,32,4096]{2,1,0:T(8,128)}, u32[]{:S(2)}) %copy-start.1) | copy-done | bytes 524312
  2.1 0.0 copy-start.2
  2.1 0.7 %copy-done.2 = f32[1,32,64]{2,1,0:T(8,128)S(1)} copy-done((f32[1,32,64]{2,1,0:T(8,128)S(1)}, f32[1,32,64]{2,1,0:T(8,128)}, u32[]{:S(2)}) %copy-start.2) | copy-done | bytes 8216
  2.8 0.0 copy-start.3
  2.8 0.7 %copy-done.3 = f32[1,32,64]{2,1,0:T(8,128)S(1)} copy-done((f32[1,32,64]{2,1,0:T(8,128)S(1)}, f32[1,32,64]{2,1,0:T(8,128)}, u32[]{:S(2)}) %copy-start.3) | copy-done | bytes 8216
  3.5 0.0 copy-start.4
  3.5 0.7 %copy-done.4 = f32[1,32,64]{2,1,0:T(8,128)S(1)} copy-done((f32[1,32,64]{2,1,0:T(8,128)S(1)}, f32[1,32,64]{2,1,0:T(8,128)}, u32[]{:S(2)}) %copy-start.4) | copy-done | bytes 8216
  4.2 0.0 copy-start.5
  4.2 0.7 %copy-done.5 = f32[1,32,64]{2,1,0:T(8,128)S(1)} copy-done((f32[1,32,64]{2,1,0:T(8,128)S(1)}, f32[1,32,64]{2,1,0:T(8,128)}, u32[]{:S(2)}) %copy-start.5) | copy-done | bytes 8216
  5.0 0.0 copy-start.6
  5.0 0.7 %copy-done.6 = f32[1,32,64]{2,1,0:T(8,128)S(1)} copy-done((f32[1,32,64]{2,1,0:T(8,128)S(1)}, f32[1,32,64]{2,1,0:T(8,128)}, u32[]{:S(2)}) %copy-start.6) | copy-done | bytes 8216
  5.7 0.0 copy-start.7
  5.7 0.7 %copy-done.7 = s32[8,8]{1,0:T(8,128)S(1)} copy-done((s32[8,8]{1,0:T(8,128)S(1)}, s32[8,8]{1,0:T(8,128)}, u32[]{:S(2)}) %copy-start.7) | copy-done | bytes 280
  6.4 0.0 copy-start.8
  6.4 0.7 %copy-done.8 = s32[1,4]{1,0:T(1,128)S(1)} copy-done((s32[1,4]{1,0:T(1,128)S(1)}, s32[1,4]{1,0:T(1,128)}, u32[]{:S(2)}) %copy-start.8) | copy-done | bytes 40
  7.0 27.8 %shard_map.91 = f32[1,32,64]{2,1,0:T(8,128)S(1)} custom-call(f32[1,32,64]{2,1,0:T(8,128)S(1)} %copy-done.2, f32[1,32,64]{2,1,0:T(8,128)S(1)} %copy-done.3, f32[1,32,4096]{2,1,0:T(8,128)S(1)} %copy-done, s32[8,8]{1,0:T(8,128)S(1)} %copy-done.7, f32[1,32,64]{2,1,0:T(8,128)S(1)} %copy-done.4, f32[1,32,64]{2,1,0:T(8,128)S(1)} %copy-done.5, ...), custom_call_target="tpu_custom_call" | custom-call | tf_op jit(solution)/shard_map/pallas_call | solution.py:396
  34.8 0.6 %copy.11 = f32[1,32,64]{2,1,0:T(8,128)} copy(f32[1,32,64]{2,1,0:T(8,128)S(1)} %shard_map.91) | data formatting | bytes 16384
Async XLA Ops:
  0.0 1.0 %copy-start = (f32[1,32,4096]{2,1,0:T(8,128)S(1)}, f32[1,32,4096]{2,1,0:T(8,128)}, u32[]{:S(2)}) copy-start(f32[1,32,4096]{2,1,0:T(8,128)} %jac_hbm.1) | copy-start | bytes 1572868
  1.0 1.0 %copy-start.1 = (f32[1,32,4096]{2,1,0:T(8,128)S(1)}, f32[1,32,4096]{2,1,0:T(8,128)}, u32[]{:S(2)}) copy-start(f32[1,32,4096]{2,1,0:T(8,128)} %factor_hbm.1) | copy-start | bytes 1572868
  2.1 0.7 %copy-start.2 = (f32[1,32,64]{2,1,0:T(8,128)S(1)}, f32[1,32,64]{2,1,0:T(8,128)}, u32[]{:S(2)}) copy-start(f32[1,32,64]{2,1,0:T(8,128)} %dens_ref.1) | copy-start | bytes 24580
  2.8 0.7 %copy-start.3 = (f32[1,32,64]{2,1,0:T(8,128)S(1)}, f32[1,32,64]{2,1,0:T(8,128)}, u32[]{:S(2)}) copy-start(f32[1,32,64]{2,1,0:T(8,128)} %source_ref.1) | copy-start | bytes 24580
  3.5 0.7 %copy-start.4 = (f32[1,32,64]{2,1,0:T(8,128)S(1)}, f32[1,32,64]{2,1,0:T(8,128)}, u32[]{:S(2)}) copy-start(f32[1,32,64]{2,1,0:T(8,128)} %transport_ref.1) | copy-start | bytes 24580
  4.2 0.7 %copy-start.5 = (f32[1,32,64]{2,1,0:T(8,128)S(1)}, f32[1,32,64]{2,1,0:T(8,128)}, u32[]{:S(2)}) copy-start(f32[1,32,64]{2,1,0:T(8,128)} %lateral_ref.1) | copy-start | bytes 24580
  5.0 0.7 %copy-start.6 = (f32[1,32,64]{2,1,0:T(8,128)S(1)}, f32[1,32,64]{2,1,0:T(8,128)}, u32[]{:S(2)}) copy-start(f32[1,32,64]{2,1,0:T(8,128)} %coupling_ref.1) | copy-start | bytes 24580
  5.7 0.7 %copy-start.7 = (s32[8,8]{1,0:T(8,128)S(1)}, s32[8,8]{1,0:T(8,128)}, u32[]{:S(2)}) copy-start(s32[8,8]{1,0:T(8,128)} %pattern_ref.1) | copy-start | bytes 772
  6.4 0.7 %copy-start.8 = (s32[1,4]{1,0:T(1,128)S(1)}, s32[1,4]{1,0:T(1,128)}, u32[]{:S(2)}) copy-start(s32[1,4]{1,0:T(1,128)} %neighbours_ref.1) | copy-start | bytes 52
